TPU v7x, 256 devices: a whole 4x4x8 slice. The times are simulated.
256 devices in a mesh: group: 4 (over y), section: 2 (over z_lo), tp: 32 (over z_hi, x, core).
Axes of the slice: x: 4, y: 4, z: 8 (z_hi: 4, z_lo: 2; z = z_hi * 2 + z_lo), core: 2. Of those that a mesh axis runs over, the one named last changes fastest.
Arguments:
- inputs: bfloat16 [1024, 6144], P(('group', 'tp')), may hold values from -6 to 6
- lengths: int32 [4], P('group'), may hold values from 1 to 256
- norm_gain: float32 [2, 6144], P('section'), may hold values from 0.1 to 1.9
- base_weight: bfloat16 [2, 2, 6144, 14336], P('section', None, None, 'tp'), may hold values from -0.078125 to 0.078125
- factor_p: bfloat16 [2, 2, 64, 6144], P('section', None, 'group', 'tp'), may hold values from -0.119628906 to 0.119628906
- factor_q: bfloat16 [2, 2, 64, 14336], P('section', None, 'group', 'tp'), may hold values from -0.119628906 to 0.119628906
Outputs:
- mixed: bfloat16 [2, 1024, 6144], P('section', ('group', 'tp'))
All inputs are finite; a program needn't handle non-finite values.
Results may differ from a plain program's by a relative error of at most 0.024.
Values may be sent and summed in bfloat16 or wider, within the bound.
A program may use at most 128 MiB of HBM per device.

v0:
```python
import jax
import jax.numpy as jnp
from jax import lax
from jax.sharding import PartitionSpec as P

adapter_scale = 2.0
norm_eps = 1e-05


def passed_along(block, axis, distance):
    devices = range(lax.axis_size(axis))
    route = [(i - distance, i) for i in devices if i - distance in devices]
    return lax.ppermute(block, axis, route)


def merge_weight(frozen_matrix, left, right):
    adapter_update = lax.dot_general(
        left, right, (((0,), (0,)), ((), ())), preferred_element_type=jnp.float32
    )
    return (frozen_matrix.astype(jnp.float32) + adapter_scale * adapter_update).astype(jnp.bfloat16)


def body(inputs, lengths, norm_gain, base_weight, factor_p, factor_q):
    section_index = lax.axis_index("section")
    tp_count = lax.axis_size("tp")
    ranked_p, full_q = (
        lax.all_gather(factor_p, "group", axis=2, tiled=True),
        lax.all_gather(factor_q, "group", axis=2, tiled=True),
    )
    full_p = lax.all_gather(ranked_p, "tp", axis=3, tiled=True)
    merged_up = merge_weight(base_weight[0, 0], full_p[0, 0], full_q[0, 0])
    merged_down = merge_weight(base_weight[0, 1], full_p[0, 1], full_q[0, 1])
    gain = norm_gain[0]
    tok_dev = inputs.shape[0]
    group_rows = tok_dev * tp_count
    seq_len = group_rows // lengths.shape[0]
    token_position = jnp.arange(group_rows, dtype=jnp.int32) % seq_len
    valid = (token_position < jnp.repeat(lengths, seq_len)).astype(jnp.float32)
    block_total = 1
    block_rows = tok_dev // block_total
    valid_blocks = valid.reshape(tp_count, block_total, block_rows)
    received = jnp.zeros((block_rows, inputs.shape[1]), jnp.bfloat16)
    results = []
    for turn_index in range(block_total + 1):
        state_block = jnp.where(section_index == 0, inputs, received)
        picked_index = jnp.clip(turn_index - section_index, 0, block_total - 1)
        keep_all = lax.dynamic_index_in_dim(valid_blocks, picked_index, 1, keepdims=False).reshape(
            -1
        )
        resid = state_block.astype(jnp.float32)
        mean_square = jnp.mean(resid * resid, axis=-1, keepdims=True)
        normed = (resid * lax.rsqrt(mean_square + norm_eps) * gain).astype(jnp.bfloat16)
        before = jnp.dot(
            lax.all_gather(normed, "tp", axis=0, tiled=True),
            merged_up,
            preferred_element_type=jnp.float32,
        )
        hidden_rows = (jax.nn.silu(before) * keep_all[:, None]).astype(jnp.bfloat16)
        summed = lax.psum_scatter(
            lax.dot_general(
                hidden_rows,
                merged_down,
                (((1,), (1,)), ((), ())),
                preferred_element_type=jnp.float32,
            ).astype(jnp.bfloat16),
            "tp",
            scatter_dimension=0,
            tiled=True,
        ).astype(jnp.float32)
        result = (resid + summed).astype(jnp.bfloat16)
        results.append(result)
        if turn_index < block_total:
            received = passed_along(result, "section", 1)
    chosen = jnp.where(section_index == 0, results[0], results[1])
    return chosen[None]


def solution(mesh):
    return jax.shard_map(
        body,
        mesh=mesh,
        in_specs=(
            P(("group", "tp"), None),
            P("group"),
            P("section", None),
            P("section", None, None, "tp"),
            P("section", None, "group", "tp"),
            P("section", None, "group", "tp"),
        ),
        out_specs=P("section", ("group", "tp"), None),
        check_vma=False,
    )
```

profile of v0, /device:TPU:33, one launch (start us, length us, event | category | flops | bytes accessed | tf_op | source)
XLA Modules:
  0.0 417.8 jit_solution(17756359295991887369)
XLA Ops:
  6.5 0.0 all-gather.6.cloned.1.call-start
  6.5 0.7 copy.11
  7.3 9.6 %all_gather.16 = bf16[1,2,64,192]{3,1,0,2:T(2,128)(2,1)S(1)} all-gather(bf16[1,2,16,192]{3,1,0,2:T(2,128)(2,1)S(1)} %copy.11), channel_id=1, replica_groups=mesh['group'=4,'section'=2,'tp'=32] {'group'}, dimensions={2}, use_global_device_ids=true | all-gather | bytes 61440 | tf_op jit(solution)/shard_map/all_gather | solution.py:27
  16.8 0.8 copy.12
  17.6 0.0 all-gather.6.cloned.1.call-update
  17.6 0.0 all-gather.4.cloned.1.call-start
  17.7 0.2 fusion.8
  17.9 1.5 fusion.10
  19.3 0.0 all-gather.4.cloned.1.call-update
  19.4 0.0 reduce-scatter.3.cloned.1.call-start
  20.1 9.3 %all_gather.18 = bf16[1,2,64,448]{3,2,1,0:T(8,128)(2,1)S(1)} all-gather(bf16[1,2,16,448]{3,2,1,0:T(8,128)(2,1)} %param.11), channel_id=1, replica_groups=mesh['group'=4,'section'=2,'tp'=32] {'group'}, dimensions={2}, use_global_device_ids=true | all-gather | bytes 143360 | tf_op jit(solution)/shard_map/all_gather | solution.py:28
  29.4 49.5 %all-gather.6.cloned.1.call-done = bf16[1,2,64,6144]{2,1,0,3:T(2,128)(2,1)} async-done(((bf16[1,2,64,192]{2,1,0,3:T(2,128)(2,1)}), bf16[1,2,64,6144]{2,1,0,3:T(2,128)(2,1)}) %all-gather.6.cloned.1.call-update) | async-done | bytes 1572880 | tf_op jit(solution)/shard_map/all_gather | solution.py:30
  78.9 8.9 %fusion.20 = (bf16[1,1,64,6144]{2,1,0,3:T(2,128)(2,1)}, bf16[1,1,64,6144]{2,1,0,3:T(2,128)(2,1)S(1)}) fusion(bf16[1,2,64,6144]{2,1,0,3:T(2,128)(2,1)} %all-gather.6.cloned.1.call-done), kind=kLoop, calls=%fused_computation.40 | loop fusion | bytes 3145728 | tf_op jit(solution)/shard_map/slice | solution.py:31
  87.8 7.1 %copy.15 = bf16[1,1,64,6144]{3,2,1,0:T(8,128)(2,1)} copy(bf16[1,1,64,6144]{2,1,0,3:T(2,128)(2,1)} %get-tuple-element.7) | data formatting | bytes 1572864
  94.9 4.9 %copy.16 = bf16[1,1,64,6144]{3,2,1,0:T(8,128)(2,1)} copy(bf16[1,1,64,6144]{2,1,0,3:T(2,128)(2,1)S(1)} %get-tuple-element.8) | data formatting | bytes 1572864
  99.8 0.0 copy-start.1
  99.8 7.0 %fusion = bf16[6144,448]{0,1:T(8,128)(2,1)} fusion(bf16[1,2,6144,448]{2,3,1,0:T(8,128)(2,1)} %param.9, bf16[1,1,64,6144]{3,2,1,0:T(8,128)(2,1)} %copy.16, bf16[1,2,64,448]{3,2,1,0:T(8,128)(2,1)S(1)} %all_gather.18), kind=kOutput, calls=%fused_computation.1 | convolution fusion | flops 363331584 | bytes 11862016 | tf_op jit(solution)/shard_map/dot_general | solution.py:17
  106.8 0.0 copy-done.1
  106.8 5.3 %fusion.1 = bf16[6144,448]{0,1:T(8,128)(2,1)} fusion(bf16[1,2,6144,448]{2,3,1,0:T(8,128)(2,1)} %param.9, bf16[1,1,64,6144]{3,2,1,0:T(8,128)(2,1)S(1)} %copy-done.1, bf16[1,2,64,448]{3,2,1,0:T(8,128)(2,1)S(1)} %all_gather.18), kind=kOutput, calls=%fused_computation.3 | convolution fusion | flops 363331584 | bytes 11862016 | tf_op jit(solution)/shard_map/dot_general | solution.py:17
  112.1 0.0 copy-start
  112.1 0.0 copy-start.2
  112.1 24.2 %all-gather.4.cloned.1.call-done = bf16[256,6144]{1,0:T(8,128)(2,1)} async-done(((bf16[8,6144]{1,0:T(8,128)(2,1)}), bf16[256,6144]{1,0:T(8,128)(2,1)}) %all-gather.4.cloned.1.call-update) | async-done | bytes 3145744 | tf_op jit(solution)/shard_map/all_gather | solution.py:54
  136.3 13.0 %convolution_convert_fusion.1 = bf16[256,6144]{1,0:T(8,128)(2,1)} fusion(bf16[6144,448]{0,1:T(8,128)(2,1)} %fusion, f32[256]{0:T(256)S(1)} %compare_convert_fusion, bf16[256,6144]{1,0:T(8,128)(2,1)} %all-gather.4.cloned.1.call-done, bf16[6144,448]{0,1:T(8,128)(2,1)} %fusion.1), kind=kOutput, calls=%fused_computation.5 | convolution fusion | flops 2820833280 | bytes 17302528 | tf_op jit(solution)/shard_map/dot_general | solution.py:60
  149.3 0.0 reduce-scatter.3.cloned.1.call-update
  149.3 0.0 all-gather.8.cloned.1.call-start
  149.3 91.2 %reduce-scatter.3.cloned.1.call-done = bf16[8,6144]{1,0:T(8,128)(2,1)} async-done(((bf16[256,6144]{1,0:T(8,128)(2,1)}), bf16[8,6144]{1,0:T(8,128)(2,1)}) %reduce-scatter.3.cloned.1.call-update) | async-done | bytes 98320 | tf_op jit(solution)/shard_map/reduce_scatter | solution.py:59
  240.5 0.0 copy-done
  240.5 0.9 fusion.11
  241.4 1.3 collective-permute-start
  242.7 4.1 collective-permute-done
  246.8 0.2 fusion.12
  247.0 0.0 copy-done.2
  247.0 0.7 fusion.14
  247.7 0.0 all-gather.8.cloned.1.call-update
  247.7 0.2 reduce-scatter.5.cloned.1.call-start
  248.0 57.2 %all-gather.8.cloned.1.call-done = bf16[256,6144]{1,0:T(8,128)(2,1)} async-done(((bf16[8,6144]{1,0:T(8,128)(2,1)}), bf16[256,6144]{1,0:T(8,128)(2,1)}) %all-gather.8.cloned.1.call-update) | async-done | bytes 3145744 | tf_op jit(solution)/shard_map/all_gather | solution.py:54
  305.2 13.1 %convolution_convert_fusion = bf16[256,6144]{1,0:T(8,128)(2,1)} fusion(bf16[6144,448]{0,1:T(8,128)(2,1)} %fusion, f32[256]{0:T(256)S(1)} %compare_convert_fusion, bf16[256,6144]{1,0:T(8,128)(2,1)} %all-gather.8.cloned.1.call-done, bf16[6144,448]{0,1:T(8,128)(2,1)} %fusion.1), kind=kOutput, calls=%fused_computation.4 | convolution fusion | flops 2820833280 | bytes 17302528 | tf_op jit(solution)/shard_map/dot_general | solution.py:60
  318.3 0.0 reduce-scatter.5.cloned.1.call-update
  318.3 91.4 %reduce-scatter.5.cloned.1.call-done = bf16[8,6144]{1,0:T(8,128)(2,1)} async-done(((bf16[256,6144]{1,0:T(8,128)(2,1)}), bf16[8,6144]{1,0:T(8,128)(2,1)}) %reduce-scatter.5.cloned.1.call-update) | async-done | bytes 98320 | tf_op jit(solution)/shard_map/reduce_scatter | solution.py:59
  409.7 1.6 fusion.17
  (3 shorter events, 0.0 us)
Async XLA Ops:
  6.5 72.4 %all-gather.6.cloned.1.call-start = ((), (), s32[]{:S(2)}) async-start(), calls=%async_computation.3 | async-start | bytes 3244032 | tf_op jit(solution)/shard_map/all_gather | solution.py:30
  17.6 118.7 %all-gather.4.cloned.1.call-start = ((), (), s32[]{:S(2)}) async-start(), calls=%async_computation.2 | async-start | bytes 3244032 | tf_op jit(solution)/shard_map/all_gather | solution.py:54
  19.4 221.1 %reduce-scatter.3.cloned.1.call-start = ((), (), s32[]{:S(2)}) async-start(), calls=%async_computation.4 | async-start | bytes 3244032 | tf_op jit(solution)/shard_map/reduce_scatter | solution.py:59
  99.8 7.0 %copy-start.1 = (bf16[1,1,64,6144]{3,2,1,0:T(8,128)(2,1)S(1)}, bf16[1,1,64,6144]{3,2,1,0:T(8,128)(2,1)}, u32[]{:S(2)}) copy-start(bf16[1,1,64,6144]{3,2,1,0:T(8,128)(2,1)} %copy.15) | copy-start | bytes 2359300
  112.1 128.4 %copy-start = (bf16[8,6144]{1,0:T(8,128)(2,1)S(1)}, bf16[8,6144]{1,0:T(8,128)(2,1)}, u32[]{:S(2)}) copy-start(bf16[8,6144]{1,0:T(8,128)(2,1)} %param.6) | copy-start | bytes 294916
  112.1 134.9 %copy-start.2 = (f32[1,6144]{1,0:T(1,128)S(1)}, f32[1,6144]{1,0:T(1,128)}, u32[]{:S(2)}) copy-start(f32[1,6144]{1,0:T(1,128)} %param.8) | copy-start | bytes 73732
  149.3 155.9 %all-gather.8.cloned.1.call-start = ((), (), s32[]{:S(2)}) async-start(), calls=%async_computation.5 | async-start | bytes 3244032 | tf_op jit(solution)/shard_map/all_gather | solution.py:54
  241.4 5.4 %collective-permute-start = (bf16[8,6144]{1,0:T(8,128)(2,1)S(1)}, bf16[8,6144]{1,0:T(8,128)(2,1)S(1)}, u32[]{:S(2)}, u32[]{:S(2)}) collective-permute-start(bf16[8,6144]{1,0:T(8,128)(2,1)S(1)} %fusion.11), channel_id=1, source_target_pairs={{0,32},{1,33},{2,34},{3,35},{4,36},{5,37},{6,38},{7,39},{8,40},{9,... | collective-permute-start | bytes 294920 | tf_op jit(solution)/shard_map/ppermute | solution.py:13
  247.7 162.0 %reduce-scatter.5.cloned.1.call-start = ((), (), s32[]{:S(2)}) async-start(), calls=%async_computation.6 | async-start | bytes 3244032 | tf_op jit(solution)/shard_map/reduce_scatter | solution.py:59
Sparse Core Ops, SparseCore 0:
  17.7 61.1 all-gather.5
  81.4 54.8 all-gather.3
  149.4 91.0 reduce-scatter.2
  247.9 57.2 all-gather.7
  318.4 91.2 reduce-scatter.4
where the time goes:
time: 422 us; the launch traced here: 418 us
  waiting for transfers between devices  318 us (75%)
  matrix products  38.3 us (9%)
  local copies, waits for them, and re-layouts  22.4 us (5%)
  blocking collectives  18.9 us (4%)
  between operations  13.8 us (3%)
  other arithmetic  5.06 us (1%)
    reduce_scatter x2, waiting for transfers between devices, body(): lax.psum_scatter(lax.dot_general(hidden_rows, merged_down, (((1,), (1,)),...  183 us
    all_gather x2, waiting for transfers between devices, body(): lax.all_gather(normed, 'tp', axis=0, tiled=True)  81.5 us
    all_gather x1, waiting for transfers between devices, body(): full_p = lax.all_gather(ranked_p, 'tp', axis=3, tiled=True)  49.5 us
    dot_general x2, matrix products, body(): lax.dot_general(hidden_rows, merged_down, (((1,), (1,)), ((), ())), prefe...  26 us
    unnamed x9, local copies, waits for them, and re-layouts  12.7 us
    dot_general x2, matrix products, merge_weight(): lax.dot_general(left, right, (((0,), (0,)), ((), ())), preferred_element_...  12.3 us
    all_gather x1, blocking collectives, body(): lax.all_gather(factor_p, 'group', axis=2, tiled=True)  9.56 us
    all_gather x1, blocking collectives, body(): lax.all_gather(factor_q, 'group', axis=2, tiled=True)  9.32 us
  transfers between devices with their start and end apart: 6, of which 6 were waited for; matrix products, arithmetic and copies ran while one was open for 8% of the time, Pallas kernels for 0%

commit v1 on v0

v1 whole, which is shorter than its diff:
```python
import functools

import jax
import jax.numpy as jnp
from jax import lax
from jax.experimental import pallas as pl
from jax.experimental.pallas import tpu as pltpu
from jax.sharding import PartitionSpec as P

adapter_scale = 2.0
norm_eps = 1e-05
NX = 4

BF, F32 = jnp.bfloat16, jnp.float32
NT = (((1,), (1,)), ((), ()))


def kernel(
    nz, nx, ng,
    x_ref, len_ref, gain_ref, w_ref, p_ref, q_ref,
    out_ref,
    st, nrm, tn, xg, wu, wd, ppad, pg, qg,
    acc, hid, usc, tsend, trecv, spart, r1, s1, r2, fs, fr, res, rsend, rrecv,
    wsem, tw_s, tw_r, ag_s, ag_r, fw_s, fw_r, pt_s, pt_r, px_s, px_r, qy_s, qy_r,
    rt_s, rt_r, rs_s, rs_r, fin_s, fin_r, rel_s, rel_r,
):
    g = lax.axis_index("group")
    sec = lax.axis_index("section")
    t = lax.axis_index("tp")
    c = lax.rem(t, 2)
    chip = lax.div(t, 2)
    xi = lax.rem(chip, nx)
    zi = lax.div(chip, nx)
    o = 1 - c
    d_model = x_ref.shape[1]
    qc = d_model // 4
    hc = d_model // 2
    rows = nz * nx * 16
    pc = d_model // (nz * nx)
    chunks = qc // pc

    def tp_of(z, x, core):
        return (z * nx + x) * 2 + core

    twin = {"tp": tp_of(zi, xi, o)}

    def xpeer(d):
        return lax.rem(xi + d, nx)

    def zpeer(d):
        return lax.rem(zi + d, nz)

    def ypeer(d):
        return lax.rem(g + d, ng)

    def to_x(d):
        return {"tp": tp_of(zi, xpeer(d), c)}

    def to_z(d):
        return {"tp": tp_of(zpeer(d), xi, c)}

    def to_y(d):
        return {"group": ypeer(d)}

    sends = []

    def rcopy(src, dst, ss, rs, dev):
        return pltpu.make_async_remote_copy(
            src_ref=src, dst_ref=dst, send_sem=ss, recv_sem=rs,
            device_id=dev, device_id_type=pl.DeviceIdType.MESH,
        )

    def go(copy):
        copy.start()
        sends.append(copy)
        return copy

    cu = pltpu.make_async_copy(w_ref.at[0, 0], wu, wsem.at[0])
    cd = pltpu.make_async_copy(w_ref.at[0, 1], wd, wsem.at[1])
    cu.start()
    cd.start()

    barrier = pltpu.get_barrier_semaphore()
    peers = [twin]
    peers += [to_x(d) for d in range(1, nx)]
    peers += [to_z(d) for d in range(1, nz)]
    peers += [to_y(d) for d in range(1, ng)]
    peers += [{"section": 1 - sec}]
    for dev in peers:
        pl.semaphore_signal(barrier, inc=1, device_id=dev, device_id_type=pl.DeviceIdType.MESH)
    pl.semaphore_wait(barrier, len(peers))

    qsends = [go(rcopy(q_ref, qg.at[:, g], qy_s.at[d - 1], qy_r.at[d - 1], to_y(d))) for d in range(1, ng)]
    qg[:, g] = q_ref[...]

    ptw = go(rcopy(p_ref, ppad, pt_s.at[0], pt_r.at[0], twin))

    def p_own():
        ptw.wait_recv()
        mine = (p_ref[...].astype(F32) + ppad[...].astype(F32)).astype(BF)
        pg[:, g, zi, xi] = mine

    pxs = [rcopy(pg.at[c, g, zi, xi], pg.at[c, g, zi, xi], px_s.at[0, d - 1], px_r.at[0, d - 1], to_x(d)) for d in range(1, nx)]
    pzs = [rcopy(pg.at[c, g, zi], pg.at[c, g, zi], px_s.at[1, d - 1], px_r.at[1, d - 1], to_z(d)) for d in range(1, nz)]
    pys = [rcopy(pg.at[c, g], pg.at[c, g], px_s.at[2, d - 1], px_r.at[2, d - 1], to_y(d)) for d in range(1, ng)]
    ptf = [rcopy(pg.at[c, lax.rem(g + d, ng)], pg.at[c, lax.rem(g + d, ng)], pt_s.at[1 + d], pt_r.at[1 + d], twin) for d in range(1, ng)]
    ptx = [
        rcopy(pg.at[c, g, zi, xpeer(d)], pg.at[c, g, zi, xpeer(d)], px_s.at[3, d - 1], px_r.at[3, d - 1], twin) for d in range(1, nx)
    ]
    ptz = [
        rcopy(pg.at[c, g, zpeer(d)], pg.at[c, g, zpeer(d)], px_s.at[4, d - 1], px_r.at[4, d - 1], twin) for d in range(1, nz)
    ]

    def start(copies):
        for k in copies:
            k.start()

    def p_x():
        start(pxs)

    def p_z():
        for k, f in zip(pxs, ptx):
            k.wait_recv()
        start(pzs)
        start(ptx)

    def p_y():
        for k in pzs:
            k.wait_recv()
        start(pys)
        start(ptz)

    def p_t():
        for k in pys:
            k.wait_recv()
        start(ptf)

    sends.extend(pxs + pzs + pys + ptf + ptx + ptz)

    p_own()
    p_x()

    relay = rcopy(rsend, rrecv, rel_s.at[0], rel_r.at[0], {"section": 1})

    @pl.when(sec == 0)
    def _():
        st[...] = x_ref[...].astype(F32)

    @pl.when(sec == 1)
    def _():
        p_z()
        p_y()
        p_t()
        relay.wait_recv()
        both = rrecv[...].astype(F32)
        st[:, :hc] = both[:8]
        st[:, hc:] = both[8:]

    resid = st[...]
    mean_square = jnp.mean(resid * resid, axis=-1, keepdims=True)
    nrm[...] = resid * lax.rsqrt(mean_square + norm_eps) * gain_ref[...]
    tw = go(rcopy(nrm, tn, tw_s.at[0], tw_r.at[0], twin))

    @pl.when(sec == 0)
    def _():
        p_z()

    tw.wait_recv()
    for q in range(4):
        cols = slice(q * qc, (q + 1) * qc)
        mine, theirs = nrm[:, cols], tn[:, cols]
        top = jnp.where(c == 0, mine, theirs)
        bottom = jnp.where(c == 0, theirs, mine)
        xg[q, zi, xi] = jnp.concatenate([top, bottom], axis=0).astype(BF)

    qa, qb = 2 * c, 2 * c + 1
    a1 = [go(rcopy(xg.at[qa, zi, xi], xg.at[qa, zi, xi], ag_s.at[0, d - 1], ag_r.at[0, d - 1], to_x(d))) for d in range(1, nx)]
    b1 = [go(rcopy(xg.at[qb, zi, xi], xg.at[qb, zi, xi], ag_s.at[1, d - 1], ag_r.at[1, d - 1], to_z(d))) for d in range(1, nz)]

    def forward(ref, i, d):
        return go(rcopy(ref, ref, fw_s.at[i, d - 1], fw_r.at[i, d - 1], twin))

    fwd = []
    for k in a1:
        k.wait_recv()
    a2 = [go(rcopy(xg.at[qa, zi], xg.at[qa, zi], ag_s.at[2, d - 1], ag_r.at[2, d - 1], to_z(d))) for d in range(1, nz)]
    for k in b1:
        k.wait_recv()
    b2 = [go(rcopy(xg.at[qb, :, xi], xg.at[qb, :, xi], ag_s.at[3, d - 1], ag_r.at[3, d - 1], to_x(d))) for d in range(1, nx)]
    for d in range(1, nx):
        fwd.append(forward(xg.at[qa, zi, lax.rem(xi + nx - d, nx)], 0, d))
    for d in range(1, nz):
        fwd.append(forward(xg.at[qb, lax.rem(zi + nz - d, nz), xi], 1, d))

    @pl.when(sec == 0)
    def _():
        p_y()

    for d in range(1, nz):
        a2[d - 1].wait_recv()
        fwd.append(forward(xg.at[qa, lax.rem(zi + nz - d, nz)], 2, d))
    for d in range(1, nx):
        b2[d - 1].wait_recv()
        fwd.append(forward(xg.at[qb, :, lax.rem(xi + nx - d, nx)], 3, d))

    cu.wait()

    def up(q):
        lhs = xg[q].reshape(rows, qc)
        return jnp.dot(lhs, wu[pl.ds(pl.multiple_of(q * qc, 128), qc), :], preferred_element_type=F32)

    acc[...] = up(qa)
    acc[...] += up(qb)

    @pl.when(sec == 0)
    def _():
        p_t()

    for k in fwd:
        k.wait_recv()
    acc[...] += up(2 * o)
    acc[...] += up(2 * o + 1)
    for k in qsends + ptf + ptx + ptz:
        k.wait_recv()

    def low(i, s):
        q = lax.div(i, chunks)
        j = lax.rem(i, chunks)
        lhs = xg[q, :, :, :, pl.ds(pl.multiple_of(j * pc, 128), pc)].reshape(rows, pc)
        z, x = lax.div(i, nx), lax.rem(i, nx)
        rhs = pg[0, :, z, x].reshape(ng * 16, pc)
        return s + lax.dot_general(lhs, rhs, NT, preferred_element_type=F32)

    s = lax.fori_loop(0, nz * nx, low, jnp.zeros((rows, ng * 16), F32))
    s_hi = s.astype(BF)
    s_lo = (s - s_hi.astype(F32)).astype(BF)
    q_up = qg[0].reshape(ng * 16, qg.shape[3])
    q_down = qg[1].reshape(ng * 16, qg.shape[3])
    low_rank = jnp.dot(s_hi, q_up, preferred_element_type=F32) + jnp.dot(s_lo, q_up, preferred_element_type=F32)
    before = acc[...] + adapter_scale * low_rank
    valid = (lax.broadcasted_iota(jnp.int32, (rows, 1), 0) < len_ref[0]).astype(F32)
    hidden = (before / (1.0 + jnp.exp(-before)) * valid).astype(BF)
    hid[...] = hidden
    usc[...] = (adapter_scale * lax.dot_general(hidden, q_down, NT, preferred_element_type=F32)).astype(BF)
    cd.wait()

    def down(i):
        at = pl.multiple_of(i * pc, 128)
        main = lax.dot_general(hid[...], wd[pl.ds(at, pc), :], NT, preferred_element_type=F32)
        z, x = lax.div(i, nx), lax.rem(i, nx)
        return main + jnp.dot(usc[...], pg[1, :, z, x].reshape(ng * 16, pc), preferred_element_type=F32)

    sent = []
    for h in range(2):
        def twin_part(j, carry, h=h):
            i = (2 * o + h) * chunks + j
            tsend[h, :, :, :, pl.ds(pl.multiple_of(j * pc, 128), pc)] = down(i).astype(BF).reshape(nz, nx, 16, pc)
            return carry

        lax.fori_loop(0, chunks, twin_part, 0)
        sent.append(go(rcopy(tsend.at[h], trecv.at[h], rt_s.at[h], rt_r.at[h], twin)))

    p1 = [[], []]
    for h in range(2):
        sent[h].wait_recv()

        def own_part(j, carry, h=h):
            i = (2 * c + h) * chunks + j
            at = pl.ds(pl.multiple_of(j * pc, 128), pc)
            both = down(i).astype(BF).astype(F32).reshape(nz, nx, 16, pc) + trecv[h, :, :, :, at].astype(F32)
            spart[h, :, :, :, at] = both.astype(BF)
            return carry

        lax.fori_loop(0, chunks, own_part, 0)
        if h == 0:
            for d in range(1, nz):
                p1[0].append(go(rcopy(spart.at[0, zpeer(d)], r1.at[0, d - 1], rs_s.at[0, d - 1], rs_r.at[0, d - 1], to_z(d))))
        else:
            for d in range(1, nx):
                p1[1].append(go(rcopy(spart.at[1, :, xpeer(d)], r1.at[1, d - 1], rs_s.at[1, d - 1], rs_r.at[1, d - 1], to_x(d))))

    p2 = [[], []]
    for h in range(2):
        for k in p1[h]:
            k.wait_recv()
        total = spart[0, zi].astype(F32) if h == 0 else spart[1, :, xi].astype(F32)
        for k in range(len(p1[h])):
            total = total + r1[h, k].astype(F32)
        s1[h] = total.astype(BF)
        if h == 0:
            for d in range(1, nx):
                p2[0].append(go(rcopy(s1.at[0, xpeer(d)], r2.at[0, d - 1], rs_s.at[2, d - 1], rs_r.at[2, d - 1], to_x(d))))
        else:
            for d in range(1, nz):
                p2[1].append(go(rcopy(s1.at[1, zpeer(d)], r2.at[1, d - 1], rs_s.at[3, d - 1], rs_r.at[3, d - 1], to_z(d))))

    for h in range(2):
        for k in p2[h]:
            k.wait_recv()
        total = s1[h, xi if h == 0 else zi].astype(F32)
        for k in range(len(p2[h])):
            total = total + r2[h, k].astype(F32)
        fs[0, :, h * qc:(h + 1) * qc] = total[:8]
        fs[1, :, h * qc:(h + 1) * qc] = total[8:]

    fin = go(rcopy(fs.at[o], fr, fin_s.at[0], fin_r.at[0], twin))
    mine_at = pl.ds(pl.multiple_of(c * hc, 128), hc)
    other_at = pl.ds(pl.multiple_of(o * hc, 128), hc)
    res[:, mine_at] = st[:, mine_at] + fs[c]
    fin.wait_recv()
    res[:, other_at] = st[:, other_at] + fr[...]
    out_ref[0] = res[...].astype(BF)

    @pl.when(sec == 0)
    def _():
        rsend[...] = jnp.concatenate([res[:, :hc], res[:, hc:]], axis=0).astype(BF)
        relay.start()
        relay.wait_send()

    for k in sends:
        k.wait_send()


def body(inputs, lengths, norm_gain, base_weight, factor_p, factor_q):
    ng = lax.axis_size("group")
    nx = NX
    nz = lax.axis_size("tp") // 2 // nx
    d_model = inputs.shape[1]
    ffw = base_weight.shape[3]
    rows = nz * nx * 16
    assert nx == nz
    qc, hc, pc = d_model // 4, d_model // 2, d_model // (nz * nx)
    core = lax.rem(lax.axis_index("tp"), 2)
    p = factor_p[0]
    blank = jnp.zeros_like(p)
    p_padded = jnp.where(
        core == 0, jnp.concatenate([p, blank], axis=2), jnp.concatenate([blank, p], axis=2)
    )
    vmem = pl.BlockSpec(memory_space=pltpu.VMEM)
    dma = pltpu.SemaphoreType.DMA
    n3 = max(nx, nz, ng) - 1
    out = pl.pallas_call(
        functools.partial(kernel, nz, nx, ng),
        out_shape=jax.ShapeDtypeStruct((1, 8, d_model), BF),
        in_specs=[
            vmem,
            pl.BlockSpec(memory_space=pltpu.SMEM),
            vmem,
            pl.BlockSpec(memory_space=pl.ANY),
            vmem,
            vmem,
        ],
        out_specs=vmem,
        scratch_shapes=[
            pltpu.VMEM((8, d_model), F32),
            pltpu.VMEM((8, d_model), F32),
            pltpu.VMEM((8, d_model), F32),
            pltpu.VMEM((4, nz, nx, 16, qc), BF),
            pltpu.VMEM((d_model, ffw), BF),
            pltpu.VMEM((d_model, ffw), BF),
            pltpu.VMEM((2, 16, pc), BF),
            pltpu.VMEM((2, ng, nz, nx, 16, pc), BF),
            pltpu.VMEM((2, ng, 16, ffw), BF),
            pltpu.VMEM((rows, ffw), F32),
            pltpu.VMEM((rows, ffw), BF),
            pltpu.VMEM((rows, ng * 16), BF),
            pltpu.VMEM((2, nz, nx, 16, qc), BF),
            pltpu.VMEM((2, nz, nx, 16, qc), BF),
            pltpu.VMEM((2, nz, nx, 16, qc), BF),
            pltpu.VMEM((2, n3, nx, 16, qc), BF),
            pltpu.VMEM((2, nx, 16, qc), BF),
            pltpu.VMEM((2, n3, 16, qc), BF),
            pltpu.VMEM((2, 8, hc), F32),
            pltpu.VMEM((8, hc), F32),
            pltpu.VMEM((8, d_model), F32),
            pltpu.VMEM((16, hc), BF),
            pltpu.VMEM((16, hc), BF),
            dma((2,)),
            dma((1,)), dma((1,)),
            dma((4, n3)), dma((4, n3)),
            dma((4, n3)), dma((4, n3)),
            dma((6,)), dma((6,)),
            dma((5, n3)), dma((5, n3)),
            dma((n3,)), dma((n3,)),
            dma((2,)), dma((2,)),
            dma((4, n3)), dma((4, n3)),
            dma((1,)), dma((1,)),
            dma((1,)), dma((1,)),
        ],
        compiler_params=pltpu.CompilerParams(
            collective_id=0, has_side_effects=True, vmem_limit_bytes=56 * 1024 * 1024
        ),
    )(inputs, lengths, norm_gain, base_weight, p_padded, factor_q[0])
    return out


def solution(mesh):
    return jax.shard_map(
        body,
        mesh=mesh,
        in_specs=(
            P(("group", "tp"), None),
            P("group"),
            P("section", None),
            P("section", None, None, "tp"),
            P("section", None, "group", "tp"),
            P("section", None, "group", "tp"),
        ),
        out_specs=P("section", ("group", "tp"), None),
        check_vma=False,
    )
```

time: 422 us -> 151 us (0.36)
  waiting for transfers between devices: 318 us -> 0 us
  Pallas kernels: 0 us -> 131 us
  matrix products: 38.3 us -> 0 us
  blocking collectives: 18.9 us -> 0 us
  between operations: 13.8 us -> 0.66 us
  local copies, waits for them, and re-layouts: 22.4 us -> 16.8 us
    reduce_scatter x2 -> x0, waiting for transfers between devices: 183 us -> none  [body(): lax.psum_scatter(lax.dot_general(hidden_rows, merged_down, (((1,), (1,)),...]
    pallas_call x0 -> x1, Pallas kernels: none -> 131 us  [body(): pl.pallas_call(functools.partial(kernel, nz, nx, ng), out_shape=jax.Shape...]
    all_gather x3 -> x0, waiting for transfers between devices: 131 us -> none  [the longest x2 81.5 us: body(): lax.all_gather(normed, 'tp', axis=0, tiled=True)]
    dot_general x4 -> x0, matrix products: 38.3 us -> none  [the longest x2 26 us: body(): lax.dot_general(hidden_rows, merged_down, (((1,), (1,)), ((), ())), prefe...]
    all_gather x2 -> x0, blocking collectives: 18.9 us -> none  [the longest x1 9.56 us: body(): lax.all_gather(factor_p, 'group', axis=2, tiled=True)]
    slice x1 -> x0, local copies, waits for them, and re-layouts: 8.91 us -> none  [body(): merged_up = merge_weight(base_weight[0, 0], full_p[0, 0], full_q[0, 0])]
    unnamed x9 -> x2, local copies, waits for them, and re-layouts: 12.7 us -> 16.8 us
  transfers between devices with their start and end apart: 6 -> 0, of which waited for: 6 -> 0; matrix products, arithmetic and copies ran while one was open for 8% -> 0% of each run, Pallas kernels for 0% -> 0%
where the time goes in v1:
time: 151 us; the launch traced here: 150 us
  Pallas kernels  131 us (87%)
  local copies, waits for them, and re-layouts  16.8 us (11%)
    pallas_call x1, Pallas kernels, body(): pl.pallas_call(functools.partial(kernel, nz, nx, ng), out_shape=jax.Shape...  131 us
    unnamed x2, local copies, waits for them, and re-layouts  16.8 us

profile of v1, /device:TPU:33, one launch (start us, length us, event | category | flops | bytes accessed | tf_op | source)
XLA Modules:
  0.0 150.0 jit_solution(7067785189662328561)
XLA Ops:
  0.7 1.5 pad_select_fusion.p_ref
  2.1 15.2 %copy.7.w_ref = bf16[1,2,6144,448]{3,2,1,0:T(8,128)(2,1)} copy(bf16[1,2,6144,448]{2,3,1,0:T(8,128)(2,1)} %param.9) | data formatting | bytes 22020096 | tf_op args[3]
  17.4 131.1 %shard_map.64 = bf16[1,8,6144]{2,1,0:T(8,128)(2,1)} custom-call(bf16[8,6144]{1,0:T(8,128)(2,1)} %x_ref.1, s32[1]{0:T(128)S(6)} %copy.9.len_ref, f32[1,6144]{1,0:T(1,128)} %gain_ref.1, bf16[1,2,6144,448]{3,2,1,0:T(8,128)(2,1)} %copy.7.w_ref, bf16[2,16,384]{2,1,0:T(8,128)(2,1)} %pad_select_fusion.p_ref, bf16[2,16,448]{2,1,0:T(8,128)(2,1)} %bitcast.2), custom_call_target="tpu_custom_call" | custom-call | tf_op jit(solution)/shard_map/pallas_call | solution.py:342
  148.4 1.5 %copy.10 = bf16[1,8,6144]{2,1,0:T(8,128)(2,1)} copy(bf16[1,8,6144]{2,1,0:T(8,128)(2,1)} %shard_map.64) | data formatting | bytes 196608

commit v2 on v0

v2 whole, which is shorter than its diff:
```python
import functools

import jax
import jax.numpy as jnp
from jax import lax
from jax.experimental import pallas as pl
from jax.experimental.pallas import tpu as pltpu
from jax.sharding import PartitionSpec as P

adapter_scale = 2.0
norm_eps = 1e-05
NX = 4

BF, F32 = jnp.bfloat16, jnp.float32
NT = (((1,), (1,)), ((), ()))
STREAMS, A = 3, 1
ORDER = (0, 1, 2)
NEAR_FIRST = (1, 3, 2)


def kernel(
    nz, nx, ng,
    x_ref, len_ref, gain_ref, w_ref, p_ref, q_ref,
    out_ref,
    xs, xt, xg, wp, psend, precv, qg, acc, hid, tsend, trecv, spart, r1, s1, r2, fb, fs, fr,
    wsem, bar_s, bar_r, g1_s, g1_r, g2_s, g2_r, f1_s, f1_r, f2_s, f2_r,
    pp_s, pp_r, pt_s, pt_r, qy_s, qy_r, rt_s, rt_r, e1_s, e1_r, e2_s, e2_r, rel_s,
):
    g = lax.axis_index("group")
    sec = lax.axis_index("section")
    t = lax.axis_index("tp")
    c = lax.rem(t, 2)
    o = 1 - c
    chip = lax.div(t, 2)
    xi = lax.rem(chip, nx)
    zi = lax.div(chip, nx)
    d_model = x_ref.shape[1]
    ffw = w_ref.shape[1]
    hc = d_model // 2
    sc = hc // STREAMS
    rows = nz * nx * 16
    pc = d_model // (nz * nx)

    def tp_of(z, x, core):
        return (z * nx + x) * 2 + core

    def xpeer(d):
        return lax.rem(xi + d, nx)

    def zpeer(d):
        return lax.rem(zi + d, nz)

    def xfrom(d):
        return lax.rem(xi + nx - d, nx)

    def zfrom(d):
        return lax.rem(zi + nz - d, nz)

    twin = {"tp": tp_of(zi, xi, o)}

    def to_x(d):
        return {"tp": tp_of(zi, xpeer(d), c)}

    def to_z(d):
        return {"tp": tp_of(zpeer(d), xi, c)}

    def to_y(d):
        return {"group": lax.rem(g + d, ng)}

    def rcopy(src, dst, ss, rs, dev):
        return pltpu.make_async_remote_copy(
            src_ref=src, dst_ref=dst, send_sem=ss, recv_sem=rs,
            device_id=dev, device_id_type=pl.DeviceIdType.MESH,
        )

    sends = []

    def go(copy):
        copy.start()
        sends.append(copy)
        return copy

    cw = [pltpu.make_async_copy(w_ref.at[k], wp.at[k, 0:ffw], wsem.at[k]) for k in range(2)]
    cw[0].start()
    cw[1].start()

    barrier = pltpu.get_barrier_semaphore()
    peers = [twin]
    peers += [to_x(d) for d in range(1, nx)]
    peers += [to_z(d) for d in range(1, nz)]
    peers += [to_y(d) for d in range(1, ng)]
    peers += [{"section": 1 - sec}]
    peers += [{"section": 1 - sec, **to_x(d)} for d in range(1, nx)]
    peers += [{"section": 1 - sec, **to_z(d)} for d in range(1, nz)]
    for dev in peers:
        pl.semaphore_signal(barrier, inc=1, device_id=dev, device_id_type=pl.DeviceIdType.MESH)

    pf = p_ref[...].astype(F32)
    blank = jnp.zeros_like(pf)
    psend[...] = jnp.where(
        c == 0, jnp.concatenate([pf, blank], axis=2), jnp.concatenate([blank, pf], axis=2)
    ).astype(BF)
    mine_at = pl.ds(pl.multiple_of(c * hc, 128), hc)
    other_at = pl.ds(pl.multiple_of(o * hc, 128), hc)
    xs[...] = x_ref[:, other_at].astype(F32)
    qg[:, g] = q_ref[...]

    pl.semaphore_wait(barrier, len(peers))

    xtw = rcopy(xs, xt, bar_s.at[0], bar_r.at[0], twin)

    @pl.when(sec == 0)
    def _():
        xtw.start()

    ptw = go(rcopy(psend, precv, bar_s.at[1], bar_r.at[1], twin))
    qsends = [go(rcopy(q_ref, qg.at[:, g], qy_s.at[d - 1], qy_r.at[d - 1], to_y(d))) for d in range(1, ng)]

    def own(s):
        return xg.at[c, s, zi, xi]

    g1 = [
        [rcopy(own(s), own(s), g1_s.at[s, d], g1_r.at[s, d], to_x(d) if s == A else to_z(d)) for d in range(nx)]
        for s in range(STREAMS)
    ]

    @pl.when(sec == 0)
    def _():
        xtw.wait_recv()
        for s in range(STREAMS):
            mine = x_ref[:, pl.ds(pl.multiple_of(c * hc + s * sc, 128), sc)].astype(F32)
            theirs = xt[:, s * sc:(s + 1) * sc]
            top = jnp.where(c == 0, mine, theirs)
            bottom = jnp.where(c == 0, theirs, mine)
            xg[c, s, zi, xi] = jnp.concatenate([top, bottom], axis=0).astype(BF)
        for s in ORDER:
            for d in range(1, nx):
                g1[s][d].start()

    ptw.wait_recv()
    piece = psend[...].astype(F32) + precv[...].astype(F32)
    gain_here = gain_ref[:, pl.ds(pl.multiple_of(chip * pc, 128), pc)]
    for k in range(2):
        scaled = piece[k] * gain_here if k == 0 else piece[k]
        wp[k, pl.ds(pl.multiple_of(ffw + g * 16, 16), 16), pl.ds(pl.multiple_of(chip * pc, 128), pc)] = scaled.astype(BF)

    def pref(group, first, width):
        return wp.at[c, pl.ds(pl.multiple_of(ffw + group * 16, 16), 16), pl.ds(pl.multiple_of(first * pc, 128), width * pc)]

    def psame(ref, i, j, dev):
        return rcopy(ref, ref, pp_s.at[i, j], pp_r.at[i, j], dev)

    px = [psame(pref(g, chip, 1), 0, d - 1, to_x(d)) for d in range(1, nx)]
    pz = [psame(pref(g, zi * nx, nx), 1, d - 1, to_z(d)) for d in range(1, nz)]
    py = [psame(pref(g, 0, nx * nz), 2, d - 1, to_y(d)) for d in range(1, ng)]
    fx = [psame(pref(g, zi * nx + xpeer(d), 1), 3, d - 1, twin) for d in range(1, nx)]
    fz = [psame(pref(g, zpeer(d) * nx, nx), 4, d - 1, twin) for d in range(1, nz)]
    fy = [psame(pref(lax.rem(g + d, ng), 0, nx * nz), 5, d - 1, twin) for d in range(1, ng)]
    sends.extend(px + pz + py + fx + fz + fy)

    def start(copies):
        for k in copies:
            k.start()

    def arrived(copies):
        for k in copies:
            k.wait_recv()

    start(px)

    def p_z():
        arrived(px)
        start(pz)
        start(fx)

    def p_y():
        arrived(pz)
        start(py)
        start(fz)

    def p_t():
        arrived(py)
        start(fy)

    def fold_gain():
        cw[0].wait()
        width = d_model // 12 if d_model % (12 * 128) == 0 else 128

        def part(j, carry):
            at = pl.ds(pl.multiple_of(j * width, 128), width)
            wp[0, 0:ffw, at] = (wp[0, 0:ffw, at].astype(F32) * gain_ref[:, at]).astype(BF)
            return carry

        lax.fori_loop(0, d_model // width, part, 0)

    @pl.when(sec == 1)
    def _():
        p_z()
        p_y()
        fold_gain()
        p_t()
        for s in range(STREAMS):
            g1[s][0].wait_recv()

    def second(s, d, e):
        ref = xg.at[c, s, zi, xfrom(d)] if s == A else xg.at[c, s, zfrom(d), xi]
        return rcopy(ref, ref, g2_s.at[s, e, d], g2_r.at[s, e, d], to_z(e) if s == A else to_x(e))

    def to_twin(s, d):
        ref = xg.at[c, s, zi, xfrom(d)] if s == A else xg.at[c, s, zfrom(d), xi]
        return rcopy(ref, ref, f1_s.at[s, d], f1_r.at[s, d], twin)

    g2 = {}
    f1, f2 = {}, {}

    def pass_on(s, d):
        for e in NEAR_FIRST:
            g2[s, d, e] = go(second(s, d, e))
        f1[s, d] = go(to_twin(s, d))

    for s in ORDER:
        pass_on(s, 0)

    @pl.when(sec == 0)
    def _():
        p_z()
        fold_gain()

    for d in NEAR_FIRST:
        for s in ORDER:
            g1[s][d].wait_recv()
            pass_on(s, d)

    @pl.when(sec == 0)
    def _():
        arrived(pz)
        start(fz)

        @pl.when(c == 0)
        def _():
            start(py)

    cw[1].wait()

    def up(h, s, total, ssq):
        lhs = xg[h, s].reshape(rows, sc)
        at = pl.ds(pl.multiple_of(h * hc + s * sc, 128), sc)
        wide = lhs.astype(F32)
        ssq = ssq + jnp.sum(wide * wide, axis=1, keepdims=True)
        part = lax.dot_general(lhs, wp[0, :, at], NT, preferred_element_type=F32)
        if total is None:
            acc[...] = part
        else:
            acc[...] += part
        return ssq

    for e in NEAR_FIRST:
        for s in ORDER:
            for d in range(nx):
                g2[s, d, e].wait_recv()
            ref = xg.at[c, s, zfrom(e)] if s == A else xg.at[c, s, :, xfrom(e)]
            f2[s, e] = go(rcopy(ref, ref, f2_s.at[s, e], f2_r.at[s, e], twin))
        if e == NEAR_FIRST[0]:

            @pl.when(sec == 0)
            def _():
                @pl.when(c == 1)
                def _():
                    start(py)

    @pl.when(sec == 0)
    def _():
        p_t()

    @pl.when(c == 1)
    def _():
        arrived(fx + fz + fy)

    ssq = jnp.zeros((rows, 1), F32)
    for n, s in enumerate(ORDER):
        ssq = up(c, s, None if n == 0 else acc, ssq)
    for s in ORDER:
        for d in range(nx):
            f1[s, d].wait_recv()
        for e in NEAR_FIRST:
            f2[s, e].wait_recv()
        ssq = up(o, s, acc, ssq)

    arrived(qsends)
    s_low = acc[:, ffw:]
    s_hi = s_low.astype(BF)
    s_lo = (s_low - s_hi.astype(F32)).astype(BF)
    q_up = qg[0].reshape(ng * 16, ffw)
    q_down = qg[1].reshape(ng * 16, ffw)
    low_rank = jnp.dot(s_hi, q_up, preferred_element_type=F32) + jnp.dot(s_lo, q_up, preferred_element_type=F32)
    row_scale = lax.rsqrt(ssq * (1.0 / d_model) + norm_eps)
    before = (acc[:, :ffw] + adapter_scale * low_rank) * row_scale
    valid = (lax.broadcasted_iota(jnp.int32, (rows, 1), 0) < len_ref[0]).astype(F32)
    hidden = (before / (1.0 + jnp.exp(-before)) * valid).astype(BF)
    hid[:, :ffw] = hidden
    hid[:, ffw:] = (adapter_scale * lax.dot_general(hidden, q_down, NT, preferred_element_type=F32)).astype(BF)

    @pl.when(c == 0)
    def _():
        arrived(fx + fz + fy)

    def down(h, s):
        at = pl.ds(pl.multiple_of(h * hc + s * sc, 128), sc)
        return jnp.dot(hid[...], wp[1, :, at], preferred_element_type=F32).astype(BF)

    rt = {}
    e1 = {}

    def twin_part(s):
        tsend[s] = down(o, s).reshape(nz, nx, 16, sc)
        rt[s] = go(rcopy(tsend.at[s], trecv.at[s], rt_s.at[s], rt_r.at[s], twin))

    def own_part(s):
        mine = down(c, s).reshape(nz, nx, 16, sc).astype(F32)
        rt[s].wait_recv()
        spart[s] = (mine + trecv[s].astype(F32)).astype(BF)
        for d in NEAR_FIRST:
            ref = spart.at[s, zpeer(d)] if s == A else spart.at[s, :, xpeer(d)]
            e1[s, d] = go(rcopy(ref, r1.at[s, d - 1], e1_s.at[s, d - 1], e1_r.at[s, d - 1], to_z(d) if s == A else to_x(d)))

    for n, s in enumerate(ORDER):
        twin_part(s)
        if n:
            own_part(ORDER[n - 1])
    own_part(ORDER[-1])

    e2 = {}
    for s in ORDER:
        total = spart[s, zi].astype(F32) if s == A else spart[s, :, xi].astype(F32)
        for d in NEAR_FIRST:
            e1[s, d].wait_recv()
            total = total + r1[s, d - 1].astype(F32)
        s1[s] = total.astype(BF)
        for d in NEAR_FIRST:
            peer = xpeer(d) if s == A else zpeer(d)
            e2[s, d] = go(rcopy(s1.at[s, peer], r2.at[s, d - 1], e2_s.at[s, d - 1], e2_r.at[s, d - 1], to_x(d) if s == A else to_z(d)))

    relay = []
    for s in ORDER:
        total = s1[s, xi if s == A else zi].astype(F32)
        for d in NEAR_FIRST:
            e2[s, d].wait_recv()
            total = total + r2[s, d - 1].astype(F32)
        total = total + xg[c, s, zi, xi].astype(F32)
        fb[s] = total.astype(BF)
        fs[0, :, s * sc:(s + 1) * sc] = total[:8]
        fs[1, :, s * sc:(s + 1) * sc] = total[8:]
        for d in range(nx):
            dev = {"section": 1, **(to_x(d) if s == A else to_z(d))}
            relay.append(rcopy(fb.at[s], own(s), rel_s.at[s, d], g1_r.at[s, d], dev))

        @pl.when(sec == 0)
        def _(s=s):
            start(relay[-nx:])

    fin = go(rcopy(fs.at[o], fr, bar_s.at[2], bar_r.at[2], twin))
    out_ref[0, :, mine_at] = fs[c].astype(BF)
    fin.wait_recv()
    out_ref[0, :, other_at] = fr[...].astype(BF)

    @pl.when(sec == 0)
    def _():
        xtw.wait_send()
        for s in range(STREAMS):
            for d in range(1, nx):
                g1[s][d].wait_send()
        for k in relay:
            k.wait_send()

    for k in sends:
        k.wait_send()


def body(inputs, lengths, norm_gain, base_weight, factor_p, factor_q):
    ng = lax.axis_size("group")
    nx = NX
    nz = lax.axis_size("tp") // 2 // nx
    assert nx == nz
    d_model = inputs.shape[1]
    ffw = base_weight.shape[3]
    rows = nz * nx * 16
    hc, pc = d_model // 2, d_model // (nz * nx)
    sc = hc // STREAMS
    vmem = pl.BlockSpec(memory_space=pltpu.VMEM)
    dma = pltpu.SemaphoreType.DMA
    n3 = max(nx, ng) - 1
    return pl.pallas_call(
        functools.partial(kernel, nz, nx, ng),
        out_shape=jax.ShapeDtypeStruct((1, 8, d_model), BF),
        in_specs=[
            vmem,
            pl.BlockSpec(memory_space=pltpu.SMEM),
            vmem,
            pl.BlockSpec(memory_space=pl.ANY),
            vmem,
            vmem,
        ],
        out_specs=vmem,
        scratch_shapes=[
            pltpu.VMEM((8, hc), F32),
            pltpu.VMEM((8, hc), F32),
            pltpu.VMEM((2, STREAMS, nz, nx, 16, sc), BF),
            pltpu.VMEM((2, ffw + ng * 16, d_model), BF),
            pltpu.VMEM((2, 16, pc), BF),
            pltpu.VMEM((2, 16, pc), BF),
            pltpu.VMEM((2, ng, 16, ffw), BF),
            pltpu.VMEM((rows, ffw + ng * 16), F32),
            pltpu.VMEM((rows, ffw + ng * 16), BF),
            pltpu.VMEM((STREAMS, nz, nx, 16, sc), BF),
            pltpu.VMEM((STREAMS, nz, nx, 16, sc), BF),
            pltpu.VMEM((STREAMS, nz, nx, 16, sc), BF),
            pltpu.VMEM((STREAMS, nx - 1, nx, 16, sc), BF),
            pltpu.VMEM((STREAMS, nx, 16, sc), BF),
            pltpu.VMEM((STREAMS, nx - 1, 16, sc), BF),
            pltpu.VMEM((STREAMS, 16, sc), BF),
            pltpu.VMEM((2, 8, hc), F32),
            pltpu.VMEM((8, hc), F32),
            dma((2,)),
            dma((3,)), dma((3,)),
            dma((STREAMS, nx)), dma((STREAMS, nx)),
            dma((STREAMS, nx, nx)), dma((STREAMS, nx, nx)),
            dma((STREAMS, nx)), dma((STREAMS, nx)),
            dma((STREAMS, nx)), dma((STREAMS, nx)),
            dma((6, n3)), dma((6, n3)),
            dma((1,)), dma((1,)),
            dma((n3,)), dma((n3,)),
            dma((STREAMS,)), dma((STREAMS,)),
            dma((STREAMS, nx)), dma((STREAMS, nx)),
            dma((STREAMS, nx)), dma((STREAMS, nx)),
            dma((STREAMS, nx)),
        ],
        compiler_params=pltpu.CompilerParams(
            collective_id=0, has_side_effects=True, vmem_limit_bytes=56 * 1024 * 1024
        ),
    )(inputs, lengths, norm_gain, jnp.swapaxes(base_weight[0], 1, 2), factor_p[0], factor_q[0])


def solution(mesh):
    return jax.shard_map(
        body,
        mesh=mesh,
        in_specs=(
            P(("group", "tp"), None),
            P("group"),
            P("section", None),
            P("section", None, None, "tp"),
            P("section", None, "group", "tp"),
            P("section", None, "group", "tp"),
        ),
        out_specs=P("section", ("group", "tp"), None),
        check_vma=False,
    )
```

time: 422 us -> 110 us (0.26)
  waiting for transfers between devices: 318 us -> 0 us
  Pallas kernels: 0 us -> 107 us
  matrix products: 38.3 us -> 0 us
  local copies, waits for them, and re-layouts: 22.4 us -> 1.54 us
  blocking collectives: 18.9 us -> 0 us
  between operations: 13.8 us -> 0.66 us
  other arithmetic: 5.06 us -> 0 us
    reduce_scatter x2 -> x0, waiting for transfers between devices: 183 us -> none  [body(): lax.psum_scatter(lax.dot_general(hidden_rows, merged_down, (((1,), (1,)),...]
    all_gather x3 -> x0, waiting for transfers between devices: 131 us -> none  [the longest x2 81.5 us: body(): lax.all_gather(normed, 'tp', axis=0, tiled=True)]
    pallas_call x0 -> x1, Pallas kernels: none -> 107 us  [body(): pl.pallas_call(functools.partial(kernel, nz, nx, ng), out_shape=jax.Shape...]
    dot_general x4 -> x0, matrix products: 38.3 us -> none  [the longest x2 26 us: body(): lax.dot_general(hidden_rows, merged_down, (((1,), (1,)), ((), ())), prefe...]
    all_gather x2 -> x0, blocking collectives: 18.9 us -> none  [the longest x1 9.56 us: body(): lax.all_gather(factor_p, 'group', axis=2, tiled=True)]
    unnamed x9 -> x1, local copies, waits for them, and re-layouts: 12.7 us -> 1.54 us
    slice x1 -> x0, local copies, waits for them, and re-layouts: 8.91 us -> none  [body(): merged_up = merge_weight(base_weight[0, 0], full_p[0, 0], full_q[0, 0])]
  transfers between devices with their start and end apart: 6 -> 0, of which waited for: 6 -> 0; matrix products, arithmetic and copies ran while one was open for 8% -> 0% of each run, Pallas kernels for 0% -> 0%
where the time goes in v2:
time: 110 us; the launch traced here: 109 us
  Pallas kernels  107 us (97%)
  local copies, waits for them, and re-layouts  1.54 us (1%)
    pallas_call x1, Pallas kernels, body(): pl.pallas_call(functools.partial(kernel, nz, nx, ng), out_shape=jax.Shape...  107 us

profile of v2, /device:TPU:33, one launch (start us, length us, event | category | flops | bytes accessed | tf_op | source)
XLA Modules:
  0.0 109.5 jit_solution(5290041575349981263)
XLA Ops:
  0.7 107.3 %shard_map.64 = bf16[1,8,6144]{2,1,0:T(8,128)(2,1)} custom-call(bf16[8,6144]{1,0:T(8,128)(2,1)} %x_ref.1, s32[1]{0:T(128)S(6)} %copy.8.len_ref, f32[1,6144]{1,0:T(1,128)} %gain_ref.1, bf16[2,448,6144]{2,1,0:T(8,128)(2,1)} %bitcast.5, bf16[2,16,192]{2,1,0:T(8,128)(2,1)} %bitcast.7, bf16[2,16,448]{2,1,0:T(8,128)(2,1)} %bitcast.6), custom_call_target="tpu_custom_call" | custom-call | tf_op jit(solution)/shard_map/pallas_call | solution.py:392
  107.9 1.5 %copy.9 = bf16[1,8,6144]{2,1,0:T(8,128)(2,1)} copy(bf16[1,8,6144]{2,1,0:T(8,128)(2,1)} %shard_map.64) | data formatting | bytes 196608

commit v3 on v0

v3 whole, which is shorter than its diff:
```python
import functools

import jax
import jax.numpy as jnp
from jax import lax
from jax.experimental import pallas as pl
from jax.experimental.pallas import tpu as pltpu
from jax.sharding import PartitionSpec as P

adapter_scale = 2.0
norm_eps = 1e-05
NX = 4

BF, F32 = jnp.bfloat16, jnp.float32
NT = (((1,), (1,)), ((), ()))
STREAMS = 4
BLOCKS = ((0, 1), (2, 3))
GATHER_A, SCATTER_A = ((1, 3), ()), ((), (1, 3))
RELAYED_GATHER, RELAYED_SUM = ((0, 1, 2, 3),) * 2, ((0, 1, 2, 3),) * 2
NEAR_FIRST = (1, 3, 2)
PIECES = (0, 1, 3, 2)


def kernel(
    nz, nx, ng,
    x_ref, len_ref, gain_ref, w_ref, p_ref, q_ref,
    out_ref,
    xs, xt, xg, wp, psend, precv, qg, acc, hid, tsend, trecv, spart, far, r1, s1, r2, fb, fs, fr, low_send, low_recv, u_send, u_recv,
    wsem, bar_s, bar_r, g1_s, g1_r, g2_s, g2_r, f1_s, f1_r, f2_s, f2_r,
    pz_s, pz_r, px_s, px_r, py_s, py_r, low_s, low_r, qy_s, qy_r, rt_s, rt_r, e1_s, e1_r, e2_s, e2_r, rel_s,
):
    g = lax.axis_index("group")
    sec = lax.axis_index("section")
    t = lax.axis_index("tp")
    c = lax.rem(t, 2)
    o = 1 - c
    chip = lax.div(t, 2)
    xi = lax.rem(chip, nx)
    zi = lax.div(chip, nx)
    d_model = x_ref.shape[1]
    ffw = w_ref.shape[1]
    hc = d_model // 2
    kc = hc // 2
    sc = kc // 2
    chips = nz * nx
    rows = chips * 8
    pc = d_model // chips

    def tp_of(z, x, core):
        return (z * nx + x) * 2 + core

    xpeers = [lax.rem(xi + d, nx) for d in range(nx)]
    zpeers = [lax.rem(zi + d, nz) for d in range(nz)]
    xfroms = [lax.rem(xi + nx - d, nx) for d in range(nx)]
    zfroms = [lax.rem(zi + nz - d, nz) for d in range(nz)]
    twin = {"tp": tp_of(zi, xi, o)}
    to_x = [{"tp": tp_of(zi, xpeers[d], c)} for d in range(nx)]
    to_z = [{"tp": tp_of(zpeers[d], xi, c)} for d in range(nz)]
    to_y = [{"group": lax.rem(g + d, ng)} for d in range(ng)]
    sec0, sec1 = sec == 0, sec == 1

    def rcopy(src, dst, ss, rs, dev):
        return pltpu.make_async_remote_copy(
            src_ref=src, dst_ref=dst, send_sem=ss, recv_sem=rs,
            device_id=dev, device_id_type=pl.DeviceIdType.MESH,
        )

    def start(copies):
        for k in copies:
            k.start()

    def arrived(copies):
        for k in copies:
            k.wait_recv()

    cw = [pltpu.make_async_copy(w_ref.at[k], wp.at[k, 0:ffw], wsem.at[k]) for k in range(2)]
    start(cw)

    barrier = pltpu.get_barrier_semaphore()
    peers = [twin, *to_x[1:], *to_z[1:], *to_y[1:], {"section": 1 - sec}]
    peers += [{"section": 1 - sec, **dev} for dev in to_x[1:] + to_z[1:]]
    for dev in peers:
        pl.semaphore_signal(barrier, inc=1, device_id=dev, device_id_type=pl.DeviceIdType.MESH)

    pf = p_ref[...].astype(F32)
    blank = jnp.zeros_like(pf)
    psend[...] = jnp.where(
        c == 0, jnp.concatenate([pf, blank], axis=2), jnp.concatenate([blank, pf], axis=2)
    ).astype(BF)
    mine_at = pl.ds(pl.multiple_of(c * hc, 128), hc)
    other_at = pl.ds(pl.multiple_of(o * hc, 128), hc)
    xs[...] = x_ref[:, other_at].astype(F32)
    qg[:, g] = q_ref[...]

    xtw = rcopy(xs, xt, bar_s.at[0], bar_r.at[0], twin)
    ptw = rcopy(psend, precv, bar_s.at[1], bar_r.at[1], twin)
    qsends = [rcopy(q_ref, qg.at[:, g], qy_s.at[d - 1], qy_r.at[d - 1], to_y[d]) for d in range(1, ng)]

    zh = nz // 2
    is_source = lax.div(zi, zh) == c

    def p_rows(group):
        return pl.ds(pl.multiple_of(ffw + group * 16, 16), 16)

    def p_piece(m):
        return wp.at[:, p_rows(g), pl.ds(pl.multiple_of(((c * zh + m) * nx + xi) * pc, 128), pc)]

    mine = lax.rem(zi, zh)
    pz = [rcopy(p_piece(mine), p_piece(mine), pz_s.at[d - 1], pz_r.at[mine], to_z[d]) for d in range(1, nz)]
    pz_in = [rcopy(p_piece(m), p_piece(m), pz_s.at[0], pz_r.at[m], to_z[1]) for m in range(zh)]
    px = [
        rcopy(p_piece(m), p_piece(m), px_s.at[d - 1, m], px_r.at[d - 1, m], to_x[d])
        for d in range(1, nx) for m in range(zh)
    ]
    py = [[], []]
    for k in range(2):
        ref = wp.at[k, p_rows(g), mine_at]
        py[k] = [rcopy(ref, ref, py_s.at[k, e - 1], py_r.at[k, e - 1], to_y[e]) for e in range(1, ng)]

    def p_z():
        @pl.when(is_source)
        def _():
            start(pz)

    def p_x():
        for m in range(zh):
            @pl.when(zi != c * zh + m)
            def _(m=m):
                pz_in[m].wait_recv()

        start(px)

    def p_y():
        arrived(px)
        start(py[0] + py[1])

    pl.semaphore_wait(barrier, len(peers))

    @pl.when(sec0)
    def _():
        xtw.start()

    ptw.start()
    start(qsends)

    ptw.wait_recv()
    piece = psend[...].astype(F32) + precv[...].astype(F32)
    gain_here = gain_ref[:, pl.ds(pl.multiple_of(chip * pc, 128), pc)]
    for k in range(2):
        scaled = piece[k] * gain_here if k == 0 else piece[k]
        wp[k, pl.ds(pl.multiple_of(ffw + g * 16, 16), 16), pl.ds(pl.multiple_of(chip * pc, 128), pc)] = scaled.astype(BF)
    p_z()

    def fold_gain():
        cw[0].wait()
        width = d_model // 12 if d_model % (12 * 128) == 0 else 128

        def fold(j, carry):
            at = pl.ds(pl.multiple_of(j * width, 128), width)
            wp[0, 0:ffw, at] = (wp[0, 0:ffw, at].astype(F32) * gain_ref[:, at]).astype(BF)
            return carry

        lax.fori_loop(0, d_model // width, fold, 0)

    def run(layer):
        sends = [ptw, *qsends, *px, *py[0], *py[1]]

        def kept(copy):
            sends.append(copy)
            return copy

        def go(copy):
            copy.start()
            return kept(copy)

        ga, sa = GATHER_A[layer], SCATTER_A[layer]

        def at_first(s, d):
            return xg.at[c, s, zi, xfroms[d]] if s in ga else xg.at[c, s, zfroms[d], xi]

        def at_both(s, d, e):
            return xg.at[c, s, zfroms[e], xfroms[d]] if s in ga else xg.at[c, s, zfroms[d], xfroms[e]]

        def first_axis(s, d, a=ga):
            return to_x[d] if s in a else to_z[d]

        def second_axis(s, d, a=ga):
            return to_z[d] if s in a else to_x[d]

        def way(s, d):
            if s in ga:
                return 1 if d == 2 else 3
            return 1 if d in (0, 3) else 3

        g1, g2, g3, f1, f2 = {}, {}, {}, {}, {}
        for s in range(STREAMS):
            for d in range(nx):
                ref = at_first(s, 0)
                g1[s, d] = rcopy(ref, ref, g1_s.at[s, d], g1_r.at[s, d], first_axis(s, d))
                ref = at_first(s, d)
                for e in (1, 3):
                    g2[s, d, e] = kept(rcopy(ref, ref, g2_s.at[s, e, d], g2_r.at[s, e, d], second_axis(s, e)))
                f1[s, d] = kept(rcopy(ref, ref, f1_s.at[s, d], f1_r.at[s, d], twin))
                if s in RELAYED_GATHER[layer]:
                    e = way(s, d)
                    ref = at_both(s, d, e)
                else:
                    e = 2
                g3[s, d] = kept(rcopy(ref, ref, g2_s.at[s, 2, d], g2_r.at[s, 2, d], second_axis(s, e)))
            for e in (1, 3, 2):
                ref = xg.at[c, s, zfroms[e]] if s in ga else xg.at[c, s, :, xfroms[e]]
                f2[s, e] = kept(rcopy(ref, ref, f2_s.at[s, e], f2_r.at[s, e], twin))

        def pass_on(s, d):
            start((g2[s, d, way(s, d)], g2[s, d, 4 - way(s, d)], f1[s, d]))
            if s not in RELAYED_GATHER[layer]:
                g3[s, d].start()

        def gather_first(b):
            for d in NEAR_FIRST:
                for s in BLOCKS[b]:
                    g1[s, d].wait_recv()
                    pass_on(s, d)

        def gather_second(b):
            for d in PIECES:
                for s in BLOCKS[b]:
                    for e in (way(s, d), 4 - way(s, d)):
                        g2[s, d, e].wait_recv()
                        if e == way(s, d) and s in RELAYED_GATHER[layer]:
                            g3[s, d].start()
            for s in BLOCKS[b]:
                start((f2[s, 1], f2[s, 3]))

        def gather_far(b):
            for s in BLOCKS[b]:
                for d in PIECES:
                    g3[s, d].wait_recv()
                f2[s, 2].start()

        def own_pieces(b):
            for s in BLOCKS[b]:
                k = s % 2
                mine = x_ref[:, pl.ds(pl.multiple_of(c * hc + k * kc, 128), kc)].astype(F32)
                piece = jnp.where(c == b, mine, xt[:, k * kc:(k + 1) * kc])
                xg[c, s, zi, xi] = jnp.concatenate([piece[:, :sc], piece[:, sc:]], axis=0).astype(BF)

        def send_first(b):
            for d in NEAR_FIRST:
                for s in BLOCKS[b]:
                    g1[s, d].start()

        if layer == 0:
            xtw.wait_recv()
            own_pieces(0)
            send_first(0)
            own_pieces(1)
            for s in BLOCKS[0]:
                pass_on(s, 0)
            send_first(1)
            fold_gain()
            p_x()
            for s in BLOCKS[1]:
                pass_on(s, 0)
            gather_first(0)
            p_y()
            gather_first(1)
            gather_second(0)
            gather_second(1)
        else:
            fold_gain()
            p_x()
            p_y()
            for b in range(2):
                for s in BLOCKS[b]:
                    g1[s, 0].wait_recv()
                    pass_on(s, 0)
                gather_first(b)
                if b == 0:
                    gather_second(0)

        cw[1].wait()
        valid_to = len_ref[0]

        def columns(h, s, f):
            return pl.ds(pl.multiple_of(h * hc + s % 2 * kc + f * sc, 128), sc)

        def up(h, s, ssq, first):
            wide = xg[h, s].reshape(chips, 16, sc).astype(F32)
            for f in range(2):
                lhs = wide[:, f * 8:(f + 1) * 8].reshape(rows, sc)
                ssq = ssq + jnp.sum(lhs * lhs, axis=1, keepdims=True)
                lhs = lhs.astype(BF)
                if h is c:
                    part = lax.dot_general(lhs, wp[0, :, columns(h, s, f)], NT, preferred_element_type=F32)
                    if first and f == 0:
                        acc[...] = part
                    else:
                        acc[...] += part
                else:
                    acc[:, :ffw] += lax.dot_general(lhs, wp[0, 0:ffw, columns(h, s, f)], NT, preferred_element_type=F32)
            return ssq

        def up_block(b):
            gather_far(b)
            if b == 0:
                arrived(py[0])
            ssq = jnp.zeros((rows, 1), F32)
            for n, s in enumerate(BLOCKS[b]):
                ssq = up(c, s, ssq, n == 0)
            low_send[b] = acc[:, ffw:]
            low = go(rcopy(low_send.at[b], low_recv.at[b], low_s.at[0, b], low_r.at[0, b], twin))
            for s in BLOCKS[b]:
                arrived([f1[s, d] for d in range(nx)] + [f2[s, e] for e in (1, 3, 2)])
                ssq = up(o, s, ssq, False)
            if b == 0:
                arrived(qsends)
            low.wait_recv()
            s_low = low_send[b] + low_recv[b]
            s_hi = s_low.astype(BF)
            s_lo = (s_low - s_hi.astype(F32)).astype(BF)
            q_up = qg[0].reshape(ng * 16, ffw)
            q_down = qg[1].reshape(ng * 16, ffw)
            low_rank = jnp.dot(s_hi, q_up, preferred_element_type=F32) + jnp.dot(s_lo, q_up, preferred_element_type=F32)
            row_scale = lax.rsqrt(ssq * (1.0 / d_model) + norm_eps)
            before = (acc[:, :ffw] + adapter_scale * low_rank) * row_scale
            r = lax.broadcasted_iota(jnp.int32, (rows, 1), 0)
            position = (r - (r & 7)) * 2 + b * 8 + (r & 7)
            valid = (position < valid_to).astype(F32)
            hidden = (before / (1.0 + jnp.exp(-before)) * valid).astype(BF)
            hid[:, :ffw] = hidden
            u_send[b] = adapter_scale * lax.dot_general(hidden, q_down, NT, preferred_element_type=F32)

        def down(h, s):
            n = ffw + ng * 16 if h is c else ffw
            parts = [
                jnp.dot(hid[:, :n], wp[1, 0:n, columns(h, s, f)], preferred_element_type=F32).reshape(chips, 8, sc)
                for f in range(2)
            ]
            return jnp.concatenate(parts, axis=1).astype(BF).reshape(nz, nx, 16, sc)

        rt, e1, e2 = {}, {}, {}

        def part(s, peer, lo, hi):
            return spart.at[s, peer, lo:hi] if s in sa else spart.at[s, lo:hi, peer]

        def peer_of(s, d):
            return zpeers[d] if s in sa else xpeers[d]

        def split(s):
            return 1 if s in sa else nx // 2

        def twin_part(s):
            tsend[s] = down(o, s)
            rt[s] = go(rcopy(tsend.at[s], trecv.at[s], rt_s.at[s], rt_r.at[s], twin))

        def own_part(s):
            mine = down(c, s).astype(F32)
            rt[s].wait_recv()
            spart[s] = (mine + trecv[s].astype(F32)).astype(BF)
            m = split(s)

            def put(i, ref, dst, d):
                e1[s, i] = go(rcopy(ref, dst, e1_s.at[s, i], e1_r.at[s, i], second_axis(s, d, sa)))

            if s not in RELAYED_SUM[layer]:
                put(2, part(s, peer_of(s, 1), 0, nx), r1.at[s, 0], 1)
                put(3, part(s, peer_of(s, 3), 0, nx), r1.at[s, 1], 3)
                put(4, part(s, peer_of(s, 2), 0, nx), far.at[s], 2)
                return
            put(0, part(s, peer_of(s, 2), 0, m), far.at[s, 0:m], 1)
            put(1, part(s, peer_of(s, 2), m, nx), far.at[s, m:nx], 3)
            put(2, part(s, peer_of(s, 1), m, nx), r1.at[s, 0, m:nx], 1)
            put(3, part(s, peer_of(s, 3), 0, m), r1.at[s, 1, 0:m], 3)

        def sum_part(s):
            m = split(s)
            for i, d, lo, hi in ((0, 1, 0, m), (1, 3, m, nx)):
                e1[s, i].wait_recv()
                far[s, lo:hi] = (far[s, lo:hi].astype(F32) + part(s, peer_of(s, d), lo, hi)[...].astype(F32)).astype(BF)
                e1[s, 4 + i] = go(rcopy(far.at[s, lo:hi], r1.at[s, i, lo:hi], e1_s.at[s, 4 + i], e1_r.at[s, 4 + i], second_axis(s, d, sa)))

        def down_block(b):
            u = go(rcopy(u_send.at[b], u_recv.at[b], low_s.at[1, b], low_r.at[1, b], twin))
            for s in BLOCKS[b]:
                twin_part(s)
            u.wait_recv()
            hid[:, ffw:] = (u_send[b] + u_recv[b]).astype(BF)
            if b == 0:
                arrived(py[1])
            for s in BLOCKS[b]:
                own_part(s)

        def sum_block(b):
            for s in BLOCKS[b]:
                if s in RELAYED_SUM[layer]:
                    sum_part(s)

        def scatter_second(b):
            for s in BLOCKS[b]:
                for i in range(2, 6 if s in RELAYED_SUM[layer] else 5):
                    e1[s, i].wait_recv()
                total = spart[s, zi].astype(F32) if s in sa else spart[s, :, xi].astype(F32)
                total = total + r1[s, 0].astype(F32) + r1[s, 1].astype(F32)
                if s not in RELAYED_SUM[layer]:
                    total = total + far[s].astype(F32)
                s1[s] = total.astype(BF)
                for d in NEAR_FIRST:
                    peer = xpeers[d] if s in sa else zpeers[d]
                    e2[s, d] = go(rcopy(s1.at[s, peer], r2.at[s, d - 1], e2_s.at[s, d - 1], e2_r.at[s, d - 1], first_axis(s, d, sa)))

        relay = []

        def finish(b):
            for s in BLOCKS[b]:
                k = s % 2
                total = s1[s, xi if s in sa else zi].astype(F32)
                for d in NEAR_FIRST:
                    e2[s, d].wait_recv()
                    total = total + r2[s, d - 1].astype(F32)
                total = total + xg[c, s, zi, xi].astype(F32)
                fb[s] = total.astype(BF)
                fs[b, :, k * kc:k * kc + sc] = total[:8]
                fs[b, :, k * kc + sc:(k + 1) * kc] = total[8:]
                if layer:
                    continue
                here = [
                    rcopy(fb.at[s], at_first(s, 0), rel_s.at[s, d], g1_r.at[s, d], {"section": 1, **first_axis(s, d, GATHER_A[1])})
                    for d in range(nx)
                ]
                relay.extend(here)
                start(here)

        up_block(0)
        if layer == 1:
            gather_second(1)
        down_block(0)
        up_block(1)
        sum_block(0)
        down_block(1)
        scatter_second(0)
        sum_block(1)
        finish(0)
        scatter_second(1)
        finish(1)

        fin = go(rcopy(fs.at[o], fr, bar_s.at[2], bar_r.at[2], twin))
        out_ref[0, :, mine_at] = fs[c].astype(BF)
        fin.wait_recv()
        out_ref[0, :, other_at] = fr[...].astype(BF)
        if layer == 0:
            sends.append(xtw)
            sends.extend(g1[s, d] for s in range(STREAMS) for d in range(1, nx))
        @pl.when(is_source)
        def _():
            for k in pz:
                k.wait_send()

        for k in sends + relay:
            k.wait_send()

    @pl.when(sec0)
    def _():
        run(0)

    @pl.when(sec1)
    def _():
        run(1)


def body(inputs, lengths, norm_gain, base_weight, factor_p, factor_q):
    ng = lax.axis_size("group")
    nx = NX
    nz = lax.axis_size("tp") // 2 // nx
    assert nx == nz
    d_model = inputs.shape[1]
    ffw = base_weight.shape[3]
    rows = nz * nx * 8
    hc, pc = d_model // 2, d_model // (nz * nx)
    sc = hc // STREAMS
    vmem = pl.BlockSpec(memory_space=pltpu.VMEM)
    dma = pltpu.SemaphoreType.DMA
    n3 = max(nx, ng) - 1
    return pl.pallas_call(
        functools.partial(kernel, nz, nx, ng),
        out_shape=jax.ShapeDtypeStruct((1, 8, d_model), BF),
        in_specs=[
            vmem,
            pl.BlockSpec(memory_space=pltpu.SMEM),
            vmem,
            pl.BlockSpec(memory_space=pl.ANY),
            vmem,
            vmem,
        ],
        out_specs=vmem,
        scratch_shapes=[
            pltpu.VMEM((8, hc), F32),
            pltpu.VMEM((8, hc), F32),
            pltpu.VMEM((2, STREAMS, nz, nx, 16, sc), BF),
            pltpu.VMEM((2, ffw + ng * 16, d_model), BF),
            pltpu.VMEM((2, 16, pc), BF),
            pltpu.VMEM((2, 16, pc), BF),
            pltpu.VMEM((2, ng, 16, ffw), BF),
            pltpu.VMEM((rows, ffw + ng * 16), F32),
            pltpu.VMEM((rows, ffw + ng * 16), BF),
            pltpu.VMEM((STREAMS, nz, nx, 16, sc), BF),
            pltpu.VMEM((STREAMS, nz, nx, 16, sc), BF),
            pltpu.VMEM((STREAMS, nz, nx, 16, sc), BF),
            pltpu.VMEM((STREAMS, nx, 16, sc), BF),
            pltpu.VMEM((STREAMS, 2, nx, 16, sc), BF),
            pltpu.VMEM((STREAMS, nx, 16, sc), BF),
            pltpu.VMEM((STREAMS, nx - 1, 16, sc), BF),
            pltpu.VMEM((STREAMS, 16, sc), BF),
            pltpu.VMEM((2, 8, hc), F32),
            pltpu.VMEM((8, hc), F32),
            pltpu.VMEM((2, rows, ng * 16), F32),
            pltpu.VMEM((2, rows, ng * 16), F32),
            pltpu.VMEM((2, rows, ng * 16), F32),
            pltpu.VMEM((2, rows, ng * 16), F32),
            dma((2,)),
            dma((3,)), dma((3,)),
            dma((STREAMS, nx)), dma((STREAMS, nx)),
            dma((STREAMS, nx, nx)), dma((STREAMS, nx, nx)),
            dma((STREAMS, nx)), dma((STREAMS, nx)),
            dma((STREAMS, nx)), dma((STREAMS, nx)),
            dma((n3,)), dma((n3,)),
            dma((n3, nz // 2)), dma((n3, nz // 2)),
            dma((2, n3)), dma((2, n3)),
            dma((2, 2)), dma((2, 2)),
            dma((n3,)), dma((n3,)),
            dma((STREAMS,)), dma((STREAMS,)),
            dma((STREAMS, 6)), dma((STREAMS, 6)),
            dma((STREAMS, nx)), dma((STREAMS, nx)),
            dma((STREAMS, nx)),
        ],
        compiler_params=pltpu.CompilerParams(
            collective_id=0, has_side_effects=True, vmem_limit_bytes=56 * 1024 * 1024
        ),
    )(inputs, lengths, norm_gain, jnp.swapaxes(base_weight[0], 1, 2), factor_p[0], factor_q[0])


def solution(mesh):
    return jax.shard_map(
        body,
        mesh=mesh,
        in_specs=(
            P(("group", "tp"), None),
            P("group"),
            P("section", None),
            P("section", None, None, "tp"),
            P("section", None, "group", "tp"),
            P("section", None, "group", "tp"),
        ),
        out_specs=P("section", ("group", "tp"), None),
        check_vma=False,
    )
```

time: 422 us -> 94.6 us (0.22)
  waiting for transfers between devices: 318 us -> 0 us
  Pallas kernels: 0 us -> 92.2 us
  matrix products: 38.3 us -> 0 us
  local copies, waits for them, and re-layouts: 22.4 us -> 1.54 us
  blocking collectives: 18.9 us -> 0 us
  between operations: 13.8 us -> 0.66 us
  other arithmetic: 5.06 us -> 0 us
    reduce_scatter x2 -> x0, waiting for transfers between devices: 183 us -> none  [body(): lax.psum_scatter(lax.dot_general(hidden_rows, merged_down, (((1,), (1,)),...]
    all_gather x3 -> x0, waiting for transfers between devices: 131 us -> none  [the longest x2 81.5 us: body(): lax.all_gather(normed, 'tp', axis=0, tiled=True)]
    pallas_call x0 -> x1, Pallas kernels: none -> 92.2 us  [body(): pl.pallas_call(functools.partial(kernel, nz, nx, ng), out_shape=jax.Shape...]
    dot_general x4 -> x0, matrix products: 38.3 us -> none  [the longest x2 26 us: body(): lax.dot_general(hidden_rows, merged_down, (((1,), (1,)), ((), ())), prefe...]
    all_gather x2 -> x0, blocking collectives: 18.9 us -> none  [the longest x1 9.56 us: body(): lax.all_gather(factor_p, 'group', axis=2, tiled=True)]
    unnamed x9 -> x1, local copies, waits for them, and re-layouts: 12.7 us -> 1.54 us
    slice x1 -> x0, local copies, waits for them, and re-layouts: 8.91 us -> none  [body(): merged_up = merge_weight(base_weight[0, 0], full_p[0, 0], full_q[0, 0])]
  transfers between devices with their start and end apart: 6 -> 0, of which waited for: 6 -> 0; matrix products, arithmetic and copies ran while one was open for 8% -> 0% of each run, Pallas kernels for 0% -> 0%
where the time goes in v3:
time: 94.6 us; the launch traced here: 94.4 us
  Pallas kernels  92.2 us (97%)
  local copies, waits for them, and re-layouts  1.54 us (2%)
    pallas_call x1, Pallas kernels, body(): pl.pallas_call(functools.partial(kernel, nz, nx, ng), out_shape=jax.Shape...  92.2 us

profile of v3, /device:TPU:33, one launch (start us, length us, event | category | flops | bytes accessed | tf_op | source)
XLA Modules:
  0.0 94.4 jit_solution(3137489720342156582)
XLA Ops:
  0.7 92.2 %shard_map.64 = bf16[1,8,6144]{2,1,0:T(8,128)(2,1)} custom-call(bf16[8,6144]{1,0:T(8,128)(2,1)} %x_ref.1, s32[1]{0:T(128)S(6)} %copy.8.len_ref, f32[1,6144]{1,0:T(1,128)} %gain_ref.1, bf16[2,448,6144]{2,1,0:T(8,128)(2,1)} %bitcast.5, bf16[2,16,192]{2,1,0:T(8,128)(2,1)} %bitcast.7, bf16[2,16,448]{2,1,0:T(8,128)(2,1)} %bitcast.6), custom_call_target="tpu_custom_call" | custom-call | tf_op jit(solution)/shard_map/pallas_call | solution.py:484
  92.9 1.5 %copy.9 = bf16[1,8,6144]{2,1,0:T(8,128)(2,1)} copy(bf16[1,8,6144]{2,1,0:T(8,128)(2,1)} %shard_map.64) | data formatting | bytes 196608

commit v4 on v3

--- a/solution.py
+++ b/solution.py
@@ -405,7 +405,7 @@
                 if s not in RELAYED_SUM[layer]:
                     total = total + far[s].astype(F32)
                 s1[s] = total.astype(BF)
-                for d in NEAR_FIRST:
+                for d in (2, 1, 3):
                     peer = xpeers[d] if s in sa else zpeers[d]
                     e2[s, d] = go(rcopy(s1.at[s, peer], r2.at[s, d - 1], e2_s.at[s, d - 1], e2_r.at[s, d - 1], first_axis(s, d, sa)))
 

time: 94.6 us -> 94.1 us (level)
  no operation moved by 1% of the time
where the time goes in v4:
time: 94.1 us; the launch traced here: 94 us
  Pallas kernels  91.8 us (98%)
  local copies, waits for them, and re-layouts  1.54 us (2%)
    pallas_call x1, Pallas kernels, body(): pl.pallas_call(functools.partial(kernel, nz, nx, ng), out_shape=jax.Shape...  91.8 us

profile of v4, /device:TPU:33, one launch (start us, length us, event | category | flops | bytes accessed | tf_op | source)
XLA Modules:
  0.0 94.0 jit_solution(15953885825462594934)
XLA Ops:
  0.7 91.8 %shard_map.64 = bf16[1,8,6144]{2,1,0:T(8,128)(2,1)} custom-call(bf16[8,6144]{1,0:T(8,128)(2,1)} %x_ref.1, s32[1]{0:T(128)S(6)} %copy.8.len_ref, f32[1,6144]{1,0:T(1,128)} %gain_ref.1, bf16[2,448,6144]{2,1,0:T(8,128)(2,1)} %bitcast.5, bf16[2,16,192]{2,1,0:T(8,128)(2,1)} %bitcast.7, bf16[2,16,448]{2,1,0:T(8,128)(2,1)} %bitcast.6), custom_call_target="tpu_custom_call" | custom-call | tf_op jit(solution)/shard_map/pallas_call | solution.py:484
  92.4 1.5 %copy.9 = bf16[1,8,6144]{2,1,0:T(8,128)(2,1)} copy(bf16[1,8,6144]{2,1,0:T(8,128)(2,1)} %shard_map.64) | data formatting | bytes 196608
